TPU v7x, 256 devices: a whole 4x4x8 slice. The times are simulated.
256 devices in a mesh: row: 8 (over z), col: 16 (over x, y), rep: 2 (over core).
Axes of the slice: x: 4, y: 4, z: 8, core: 2. Of those that a mesh axis runs over, the one named last changes fastest.
Arguments:
- gradients: float32 [2, 8192, 8192], P('rep', ('row', 'col')), may hold values from -6 to 6
- momentum: float32 [8192, 8192], P(('row', 'rep'), 'col'), may hold values from -6 to 6
- right_basis: float32 [8192, 1024], P('col'), may hold values from -0.0625 to 0.0625
Outputs:
- new_momentum: float32 [8192, 8192], P(('row', 'rep'), 'col')
- new_basis: float32 [8192, 1024], P('col')
- update: float32 [8192, 8192], P(('row', 'rep'), 'col')
All inputs are finite; a program needn't handle non-finite values.
Results may differ from a plain program's by a relative error of at most 0.00014.
Values sent between devices are 32-bit elements; how exact they have to be, the bound alone decides.
A program may use at most 128 MiB of HBM per device.

v0:
```python
import math

import jax
import jax.numpy as jnp
from jax import lax
from jax.sharding import PartitionSpec as P

D = 8192
RANK = 1024


EPSILON = 1e-06
RIDGE = 0.001
DECAY = 0.95


def cross(left, right):
    return lax.dot_general(
        left,
        right,
        (((0,), (0,)), ((), ())),
        precision=lax.Precision.HIGHEST,
        preferred_element_type=jnp.float32,
    )


def outer(left, right):
    return lax.dot_general(
        left,
        right,
        (((1,), (1,)), ((), ())),
        precision=lax.Precision.HIGHEST,
        preferred_element_type=jnp.float32,
    )


def column_squares(panel):
    return jnp.sum(panel * panel, axis=0, keepdims=True)


def solve_right(factor, panel):
    return lax.linalg.triangular_solve(factor, panel, left_side=False, lower=True, transpose_a=True)


def shards(gradients, momentum, right_basis):
    slab = gradients[0]
    regrid = lax.all_to_all(slab, "col", split_axis=1, concat_axis=0, tiled=True)
    summed = lax.psum_scatter(regrid, "rep", scatter_dimension=0, tiled=True)
    buffer = momentum + summed
    partial_left = jnp.dot(
        buffer, right_basis, precision=lax.Precision.HIGHEST, preferred_element_type=jnp.float32
    )
    left_panel = lax.psum(partial_left, "col")
    ridge_eye = RIDGE * jnp.eye(left_panel.shape[1], dtype=jnp.float32)
    local_gram = cross(left_panel, left_panel)
    gram = lax.psum(local_gram, ("row", "rep"))
    factor = jnp.linalg.cholesky(gram + ridge_eye)
    left_unit = solve_right(factor, left_panel)
    partial_right = cross(buffer, left_unit)
    right_share = lax.psum_scatter(partial_right, ("row", "rep"), scatter_dimension=1, tiled=True)
    share_norm = jnp.sqrt(lax.psum(column_squares(right_share), "col") + EPSILON)
    right_panel, right_norm = (
        lax.all_gather(right_share, ("row", "rep"), axis=1, tiled=True),
        lax.all_gather(share_norm, ("row", "rep"), axis=1, tiled=True),
    )
    new_basis = right_panel / right_norm
    new_momentum = buffer - (1.0 - DECAY) * outer(left_unit, right_panel)
    scale = D / math.sqrt(RANK)
    update = scale * outer(left_unit, new_basis)
    return (new_momentum, new_basis, update)


def solution(mesh):
    return jax.shard_map(
        shards,
        mesh=mesh,
        in_specs=(P("rep", ("row", "col"), None), P(("row", "rep"), "col"), P("col", None)),
        out_specs=(P(("row", "rep"), "col"), P("col", None), P(("row", "rep"), "col")),
        check_vma=False,
    )
```

profile of v0, /device:TPU:0, one launch (start us, length us, event | category | flops | bytes accessed | tf_op | source)
XLA Modules:
  0.0 817.6 jit_solution(2948387973416063741)
XLA Ops:
  7.2 2.9 copy.34
  11.4 33.5 %all_to_all.19 = f32[64,16,512]{2,0,1:T(8,128)} all-to-all(f32[64,16,512]{2,0,1:T(8,128)S(1)} %copy.6), channel_id=1, replica_groups=mesh['row'=8,'col'=16,'rep'=2] {'col'}, dimensions={1} | all-to-all | bytes 4194304 | tf_op jit(solution)/shard_map/all_to_all | solution.py:47
  44.9 14.8 %reduce-scatter.3.cloned.1.call-done = f32[512,512]{1,0:T(8,128)} async-done(((f32[1024,512]{1,0:T(8,128)}), f32[512,512]{1,0:T(8,128)}) %reduce-scatter.3.cloned.1.call-update) | async-done | bytes 1048592 | tf_op jit(solution)/shard_map/reduce_scatter | solution.py:48
  61.5 4.9 fusion.63
  66.4 101.9 %all-reduce.5.cloned.1.call-done = f32[512,1024]{1,0:T(8,128)} async-done(((f32[512,1024]{1,0:T(8,128)}), f32[512,1024]{1,0:T(8,128)}) %all-reduce.5.cloned.1.call-update) | async-done | bytes 2097168 | tf_op jit(solution)/shard_map/psum | solution.py:53
  168.3 10.4 %fusion.64 = f32[1024,1024]{0,1:T(8,128)} fusion(f32[512,1024]{1,0:T(8,128)} %all-reduce.5.cloned.1.call-done), kind=kOutput, calls=%fused_computation.164 | convolution fusion | flops 6442450944 | bytes 6291456 | tf_op jit(solution)/shard_map/dot_general | solution.py:18
  178.8 121.0 %all-reduce.7.cloned.1.call-done = f32[1024,1024]{0,1:T(8,128)} async-done(((f32[1024,1024]{0,1:T(8,128)}), f32[1024,1024]{0,1:T(8,128)}) %all-reduce.7.cloned.1.call-update) | async-done | bytes 4194320 | tf_op jit(solution)/shard_map/psum | solution.py:56
  299.8 4.8 select_add_fusion
  304.6 5.5 copy.8
  310.1 4.5 fusion
  316.5 11.7 %cholesky.222 = f32[128,128]{1,0:T(8,128)S(1)} custom-call(f32[128,128]{1,0:T(8,128)S(1)} %cholesky.577), custom_call_target="Cholesky" | custom-call | tf_op jit(solution)/shard_map/jit(cholesky)/cholesky | solution.py:57
  328.2 9.8 %custom-call.62 = f32[1,128,128]{1,2,0:T(8,128)S(1)} custom-call(f32[1,128,128]{2,1,0:T(8,128)S(1)} %get-tuple-element.66), custom_call_target="InvertDiagBlocksLowerTriangular" | custom-call | tf_op jit(solution)/shard_map/jit(cholesky)/cholesky | solution.py:57
  341.2 11.7 %cholesky.243 = f32[128,128]{1,0:T(8,128)S(1)} custom-call(f32[128,128]{1,0:T(8,128)S(1)} %cholesky.581), custom_call_target="Cholesky" | custom-call | tf_op jit(solution)/shard_map/jit(cholesky)/cholesky | solution.py:57
  353.5 9.8 %custom-call.63 = f32[1,128,128]{1,2,0:T(8,128)S(1)} custom-call(f32[1,128,128]{2,1,0:T(8,128)S(1)} %get-tuple-element.64), custom_call_target="InvertDiagBlocksLowerTriangular" | custom-call | tf_op jit(solution)/shard_map/jit(cholesky)/cholesky | solution.py:57
  366.4 2.4 convolution_subtract_fusion.1
  368.9 11.7 %cholesky.466 = f32[128,128]{1,0:T(8,128)S(1)} custom-call(f32[128,128]{1,0:T(8,128)S(1)} %cholesky.586), custom_call_target="Cholesky" | custom-call | tf_op jit(solution)/shard_map/jit(cholesky)/cholesky | solution.py:57
  381.3 9.8 %custom-call.64 = f32[1,128,128]{1,2,0:T(8,128)S(1)} custom-call(f32[1,128,128]{2,1,0:T(8,128)S(1)} %get-tuple-element.62), custom_call_target="InvertDiagBlocksLowerTriangular" | custom-call | tf_op jit(solution)/shard_map/jit(cholesky)/cholesky | solution.py:57
  392.4 3.5 convolution_subtract_fusion.2
  396.0 11.7 %cholesky.485 = f32[128,128]{1,0:T(8,128)S(1)} custom-call(f32[128,128]{1,0:T(8,128)S(1)} %cholesky.591), custom_call_target="Cholesky" | custom-call | tf_op jit(solution)/shard_map/jit(cholesky)/cholesky | solution.py:57
  408.4 9.8 %custom-call.65 = f32[1,128,128]{1,2,0:T(8,128)S(1)} custom-call(f32[1,128,128]{2,1,0:T(8,128)S(1)} %get-tuple-element.60), custom_call_target="InvertDiagBlocksLowerTriangular" | custom-call | tf_op jit(solution)/shard_map/jit(cholesky)/cholesky | solution.py:57
  419.4 3.1 convolution_subtract_fusion.10
  422.6 11.9 %cholesky.504 = f32[128,128]{1,0:T(8,128)S(1)} custom-call(f32[128,128]{1,0:T(8,128)S(1)} %cholesky.596), custom_call_target="Cholesky" | custom-call | tf_op jit(solution)/shard_map/jit(cholesky)/cholesky | solution.py:57
  435.2 9.8 %custom-call.66 = f32[1,128,128]{1,2,0:T(8,128)S(1)} custom-call(f32[1,128,128]{2,1,0:T(8,128)S(1)} %get-tuple-element.58), custom_call_target="InvertDiagBlocksLowerTriangular" | custom-call | tf_op jit(solution)/shard_map/jit(cholesky)/cholesky | solution.py:57
  446.1 3.1 convolution_subtract_fusion.11
  449.2 11.7 %cholesky.524 = f32[128,128]{1,0:T(8,128)S(1)} custom-call(f32[128,128]{1,0:T(8,128)S(1)} %cholesky.601), custom_call_target="Cholesky" | custom-call | tf_op jit(solution)/shard_map/jit(cholesky)/cholesky | solution.py:57
  461.7 9.8 %custom-call.67 = f32[1,128,128]{1,2,0:T(8,128)S(1)} custom-call(f32[1,128,128]{2,1,0:T(8,128)S(1)} %get-tuple-element.56), custom_call_target="InvertDiagBlocksLowerTriangular" | custom-call | tf_op jit(solution)/shard_map/jit(cholesky)/cholesky | solution.py:57
  472.5 3.1 convolution_subtract_fusion.12
  475.6 11.7 %cholesky.544 = f32[128,128]{1,0:T(8,128)S(1)} custom-call(f32[128,128]{1,0:T(8,128)S(1)} %cholesky.606), custom_call_target="Cholesky" | custom-call | tf_op jit(solution)/shard_map/jit(cholesky)/cholesky | solution.py:57
  488.1 9.8 %custom-call.68 = f32[1,128,128]{1,2,0:T(8,128)S(1)} custom-call(f32[1,128,128]{2,1,0:T(8,128)S(1)} %get-tuple-element.54), custom_call_target="InvertDiagBlocksLowerTriangular" | custom-call | tf_op jit(solution)/shard_map/jit(cholesky)/cholesky | solution.py:57
  500.9 11.7 %cholesky.562 = f32[128,128]{1,0:T(8,128)S(1)} custom-call(f32[128,128]{1,0:T(8,128)S(1)} %convolution_subtract_fusion.13), custom_call_target="Cholesky" | custom-call | tf_op jit(solution)/shard_map/jit(cholesky)/cholesky | solution.py:57
  523.0 5.0 select_select_fusion
  528.0 28.7 %while.1 = (s32[]{:T(128)}, f32[1024,1024]{0,1:T(8,128)}, s32[8,2]{0,1:T(2,128)S(1)}, f32[8,128,128]{2,1,0:T(8,128)}, s32[]{:T(128)}) while((s32[]{:T(128)}, f32[1024,1024]{0,1:T(8,128)}, s32[8,2]{0,1:T(2,128)S(1)}, f32[8,128,128]{2,1,0:T(8,128)}, s32[]{:T(128)}) %tuple.55), condition=%wide.while_cond, body=%wide.while_body.sunk | while | flops 2 | bytes 393829 | solution.py:42
  528.6 2.3 dynamic-slice.8
  532.2 2.3 dynamic-slice.8
  535.8 2.3 dynamic-slice.8
  556.7 80.2 %custom-call.69 = f32[8,128,128]{1,2,0:T(8,128)} custom-call(f32[8,128,128]{2,1,0:T(8,128)} %get-tuple-element.10), custom_call_target="InvertDiagBlocksLowerTriangular" | custom-call | tf_op jit(solution)/shard_map/triangular_solve | solution.py:42
  642.6 2.4 convolution_subtract_fusion.8
  645.5 2.8 convolution_subtract_fusion.9
  648.7 3.2 convolution_subtract_fusion.4
  652.4 3.7 convolution_subtract_fusion.7
  656.7 4.1 convolution_subtract_fusion.3
  662.6 4.9 fusion.65
  667.5 59.3 %reduce-scatter.5.cloned.1.call-done = f32[512,64]{0,1:T(8,128)} async-done(((f32[512,1024]{0,1:T(8,128)}), f32[512,64]{0,1:T(8,128)}) %reduce-scatter.5.cloned.1.call-update) | async-done | bytes 131088 | tf_op jit(solution)/shard_map/reduce_scatter | solution.py:60
  729.1 40.1 %psum.23 = f32[1,64]{1,0:T(1,128)S(1)} all-reduce(f32[1,64]{1,0:T(1,128)S(1)} %bitcast.122), channel_id=1, replica_groups=mesh['row'=8,'col'=16,'rep'=2] {'col'}, use_global_device_ids=true, to_apply=%region_21.22 | all-reduce | flops 64 | bytes 512 | tf_op jit(solution)/shard_map/psum | solution.py:61
  769.3 23.5 %all-reduce.1 = f32[1024]{0:T(1024)S(1)} all-reduce(f32[1024]{0:T(1024)S(1)} %bitcast_dynamic-update-slice_fusion.1), channel_id=1, replica_groups=mesh['row'=8,'col'=16,'rep'=2] {'row','rep'}, use_global_device_ids=true, to_apply=%add.1 | all-reduce | flops 1024 | bytes 8192
  796.2 4.5 convolution_multiply_fusion
  800.7 3.2 copy.25
  803.9 6.7 fusion.1
  (137 shorter events, 64.8 us)
Async XLA Ops:
  7.2 54.3 %copy-start = (f32[512,1024]{1,0:T(8,128)S(1)}, f32[512,1024]{1,0:T(8,128)}, u32[]{:S(2)}) copy-start(f32[512,1024]{1,0:T(8,128)} %param.5) | copy-start | bytes 6291460
  7.2 52.5 %reduce-scatter.3.cloned.1.call-start = ((), (), s32[]{:S(2)}) async-start(), calls=%async_computation.3 | async-start | bytes 3145728 | tf_op jit(solution)/shard_map/reduce_scatter | solution.py:48
  44.9 123.4 %all-reduce.5.cloned.1.call-start = ((), (), s32[]{:S(2)}) async-start(), calls=%async_computation.4 | async-start | bytes 4194304 | tf_op jit(solution)/shard_map/psum | solution.py:53
  66.4 233.4 %all-reduce.7.cloned.1.call-start = ((), (), s32[]{:S(2)}) async-start(), calls=%async_computation.5 | async-start | bytes 8388608 | tf_op jit(solution)/shard_map/psum | solution.py:56
  178.7 548.1 %reduce-scatter.5.cloned.1.call-start = ((), (), s32[]{:S(2)}) async-start(), calls=%async_computation.6 | async-start | bytes 2228224 | tf_op jit(solution)/shard_map/reduce_scatter | solution.py:60
  314.6 1.9 copy-start.7
  364.5 2.0 copy-start.2
  523.0 113.9 %copy-start.3 = (f32[512,1024]{1,0:T(8,128)S(1)}, f32[512,1024]{1,0:T(8,128)}, u32[]{:S(2)}) copy-start(f32[512,1024]{1,0:T(8,128)} %all-reduce.5.cloned.1.call-done) | copy-start | bytes 6291460
  636.9 2.8 copy-start.8
  661.2 1.4 copy-start.4
  667.4 59.4 %copy-start.9 = (u32[256]{0:T(256)S(1)}, u32[256]{0:T(256)}, u32[]{:S(2)}) copy-start(u32[256]{0:T(256)} %constant.304) | copy-start | bytes 3076
  667.5 125.4 %all-gather.2.cloned.1.call-start = ((), (), s32[]{:S(2)}) async-start(), calls=%async_computation.7 | async-start | bytes 2228224 | tf_op jit(solution)/shard_map/all_gather | solution.py:63
  792.9 3.3 copy-start.5
  794.9 1.3 copy-start.6
  800.7 9.9 %copy-start.1 = (f32[512,1024]{1,0:T(8,128)S(1)}, f32[512,1024]{1,0:T(8,128)}, u32[]{:S(2)}) copy-start(f32[512,1024]{1,0:T(8,128)} %param.5) | copy-start | bytes 6291460
Sparse Core Ops, SparseCore 0:
  45.0 14.6 reduce-scatter.2
  66.5 101.7 all-reduce.4
  178.8 120.9 all-reduce.6
  667.6 59.1 reduce-scatter.4
  728.5 38.1 all-gather.1
where the time goes:
time: 829 us; the launch traced here: 818 us
  waiting for transfers between devices  297 us (36%)
  other arithmetic  267 us (32%)
  blocking collectives  97.1 us (12%)
  matrix products  81.8 us (10%)
  local copies, waits for them, and re-layouts  54.1 us (7%)
  between operations  20.6 us (2%)
    another operation x30, other arithmetic, shards(): factor = jnp.linalg.cholesky(gram + ridge_eye)  167 us
    psum x1, waiting for transfers between devices, shards(): gram = lax.psum(local_gram, ('row', 'rep'))  121 us
    psum x1, waiting for transfers between devices, shards(): left_panel = lax.psum(partial_left, 'col')  102 us
    another operation x3, other arithmetic, solve_right(): lax.linalg.triangular_solve(factor, panel, left_side=False, lower=True, t...  85.2 us
    reduce_scatter x1, waiting for transfers between devices, shards(): lax.psum_scatter(partial_right, ('row', 'rep'), scatter_dimension=1, tile...  59.3 us
    psum x1, blocking collectives, shards(): lax.psum(column_squares(right_share), 'col') + EPSILON  40.1 us
    all_to_all x1, blocking collectives, shards(): lax.all_to_all(slab, 'col', split_axis=1, concat_axis=0, tiled=True)  33.5 us
    another operation x40, local copies, waits for them, and re-layouts  28.6 us
  transfers between devices with their start and end apart: 5, of which 4 were waited for; matrix products, arithmetic and copies ran while one was open for 0% of the time, Pallas kernels for 0%

commit v1 on v0

v1 whole, which is shorter than its diff:
```python
import functools
import math

import jax, jax.numpy as jnp
from jax import lax
from jax.experimental import pallas as pl
from jax.experimental.pallas import tpu as pltpu
from jax.sharding import PartitionSpec as P

N = 1024
NB = 128
HI = lax.Precision.HIGHEST


def factor_block(rows):
    nr = len(rows)
    rows = list(rows)
    lane = lax.broadcasted_iota(jnp.int32, (8, NB), 1)
    sub = lax.broadcasted_iota(jnp.int32, (8, NB), 0)

    def lanes(v, j):
        return jnp.broadcast_to(v[:, j : j + 1], (8, NB))

    def subs(v, k):
        return jnp.broadcast_to(v[k : k + 1, :], (8, NB))

    for J in range(nr):
        blk = (lane >= 8 * J) & (lane < 8 * J + 8)
        V = rows[J]
        C = [lanes(V, 8 * J + k) for k in range(8)]
        D = {i: [lanes(rows[i], 8 * J + k) for k in range(8)] for i in range(J + 1, nr)}
        V = jnp.where(blk, jnp.where(lane - 8 * J == sub, 1.0, 0.0), V)
        for i in range(J + 1, nr):
            rows[i] = jnp.where(blk, 0.0, rows[i])
        for k in range(8):
            s = lax.rsqrt(subs(C[k], k))
            vk = subs(V, k) * s
            f = jnp.where(sub > k, C[k] * s, 0.0)
            V = jnp.where(sub == k, vk, V - f * vk)
            ck = {}
            for q in range(k + 1, 8):
                ck[q] = subs(C[q], k) * s
                C[q] = C[q] - f * ck[q]
            for i in range(J + 1, nr):
                fi = D[i][k] * s
                rows[i] = rows[i] - fi * vk
                for q in range(k + 1, 8):
                    D[i][q] = D[i][q] - fi * ck[q]
        rows[J] = V
    return rows


def chol_kernel(g_ref, x_ref, ridge, prec=HI):
    nb = N // NB
    r = lax.broadcasted_iota(jnp.int32, (NB, NB), 0)
    c = lax.broadcasted_iota(jnp.int32, (NB, NB), 1)
    x_ref[...] = g_ref[...]

    def step(k, _):
        kr = pl.ds(pl.multiple_of(k * NB, NB), NB)
        rows = [x_ref[pl.ds(pl.multiple_of(k * NB + 8 * i, 8), 8), kr] for i in range(NB // 8)]
        eye8 = [jnp.where(lax.broadcasted_iota(jnp.int32, (8, NB), 0) + 8 * i == lax.broadcasted_iota(jnp.int32, (8, NB), 1), ridge, 0.0) for i in range(NB // 8)]
        rows = [a + b for a, b in zip(rows, eye8)]
        rows = factor_block(rows)
        res = jnp.concatenate(rows, axis=0)
        dinv = jnp.where(r >= c, res, 0.0)
        x_ref[kr, kr] = jnp.where(r == c, 1.0, 0.0)
        rs = lax.dot_general(dinv, x_ref[kr, :], (((1,), (0,)), ((), ())), precision=prec, preferred_element_type=jnp.float32)
        x_ref[kr, :] = rs

        def trail(i, _):
            ir = pl.ds(pl.multiple_of(i * NB, NB), NB)
            f = x_ref[kr, ir]
            x_ref[ir, kr] = jnp.zeros((NB, NB), jnp.float32)
            x_ref[ir, :] = x_ref[ir, :] - lax.dot_general(f, x_ref[kr, :], (((0,), (0,)), ((), ())), precision=prec, preferred_element_type=jnp.float32)
            return 0

        lax.fori_loop(k + 1, nb, trail, 0)
        return 0

    lax.fori_loop(0, nb, step, 0)


def chol_inv(g, ridge):
    return pl.pallas_call(
        functools.partial(chol_kernel, ridge=ridge),
        out_shape=jax.ShapeDtypeStruct((N, N), jnp.float32),
        in_specs=[pl.BlockSpec(memory_space=pltpu.VMEM)],
        out_specs=pl.BlockSpec(memory_space=pltpu.VMEM),
        cost_estimate=pl.CostEstimate(flops=100_000_000_000, bytes_accessed=8 << 20, transcendentals=0),
        compiler_params=pltpu.CompilerParams(vmem_limit_bytes=40 << 20),
    )(g)


EPSILON = 1e-06
RIDGE = 0.001
DECAY = 0.95
D = 8192


def dot(left, right, dims, precision=HI):
    return lax.dot_general(left, right, (dims, ((), ())), precision=precision, preferred_element_type=jnp.float32)


def shards(gradients, momentum, right_basis):
    slab = gradients[0]
    regrid = lax.all_to_all(slab, "col", split_axis=1, concat_axis=0, tiled=True)
    summed = lax.psum_scatter(regrid, "rep", scatter_dimension=0, tiled=True)
    buffer = momentum + summed
    left_panel = lax.psum(dot(buffer, right_basis, ((1,), (0,))), "col")
    share = N // lax.axis_size("col")
    mine = lax.dynamic_slice_in_dim(left_panel, lax.axis_index("col") * share, share, 1)
    gram_share = lax.psum(dot(mine, left_panel, ((0,), (0,))), ("row", "rep"))
    gram = lax.all_gather(gram_share, "col", axis=0, tiled=True)
    partial_cross, gram = lax.optimization_barrier((dot(buffer, left_panel, ((0,), (0,))), gram))
    cross_panel = lax.psum(partial_cross, ("row", "rep"))
    low = jnp.tril(chol_inv(gram, RIDGE))
    left_unit = dot(left_panel, low, ((1,), (1,)))
    right_panel = dot(cross_panel, low, ((1,), (1,)))
    squares = lax.psum(jnp.sum(right_panel * right_panel, axis=0, keepdims=True), "col")
    new_basis = right_panel / jnp.sqrt(squares + EPSILON)
    new_momentum = buffer - (1.0 - DECAY) * dot(left_unit, right_panel, ((1,), (1,)))
    update = (D / math.sqrt(N)) * dot(left_unit, new_basis, ((1,), (1,)))
    return (new_momentum, new_basis, update)


def solution(mesh):
    return jax.shard_map(
        shards,
        mesh=mesh,
        in_specs=(P("rep", ("row", "col"), None), P(("row", "rep"), "col"), P("col", None)),
        out_specs=(P(("row", "rep"), "col"), P("col", None), P(("row", "rep"), "col")),
        check_vma=False,
    )
```

time: 829 us -> 528 us (0.64); the launches traced: 818 us -> 528 us
  other arithmetic: 267 us -> 2.13 us
  Pallas kernels: 0 us -> 55.3 us
  local copies, waits for them, and re-layouts: 54.1 us -> 9.49 us
  matrix products: 81.8 us -> 45.3 us
  waiting for transfers between devices: 297 us -> 328 us
  blocking collectives: 97.1 us -> 73.8 us
    another operation x33 -> x0, other arithmetic: 253 us -> none  [the longest x30 167 us: shards(): factor = jnp.linalg.cholesky(gram + ridge_eye)]
    reduce_scatter x1 -> x0, waiting for transfers between devices: 59.3 us -> none  [shards(): lax.psum_scatter(partial_right, ('row', 'rep'), scatter_dimension=1, tile...]
    pallas_call x0 -> x1, Pallas kernels: none -> 55.3 us  [chol_inv(): pl.pallas_call(functools.partial(chol_kernel, ridge=ridge), out_shape=jax...]
    all_gather x1, waiting for transfers between devices: 0.02 us -> 53 us  [shards(): gram = lax.all_gather(gram_share, 'col', axis=0, tiled=True)]
    another operation x29 -> x0, matrix products: 50.5 us -> none  [the longest x14 26.3 us: shards(): factor = jnp.linalg.cholesky(gram + ridge_eye)]
    psum x2 -> x3, waiting for transfers between devices: 223 us -> 260 us  [the longest x1 108 us: shards(): gram_share = lax.psum(dot(mine, left_panel, ((0,), (0,))), ('row', 'rep'))]
    another operation x66 -> x0, local copies, waits for them, and re-layouts: 34 us -> none
    unnamed x1 -> x0, blocking collectives: 23.5 us -> none
  transfers between devices with their start and end apart: 5 -> 5, of which waited for: 4 -> 5; matrix products, arithmetic and copies ran while one was open for 0% -> 3% of each run, Pallas kernels for 0% -> 10%
where the time goes in v1:
time: 528 us
  waiting for transfers between devices  328 us (62%)
  blocking collectives  73.8 us (14%)
  Pallas kernels  55.3 us (10%)
  matrix products  45.3 us (9%)
  between operations  13.9 us (3%)
  local copies, waits for them, and re-layouts  9.49 us (2%)
    psum x1, waiting for transfers between devices, shards(): gram_share = lax.psum(dot(mine, left_panel, ((0,), (0,))), ('row', 'rep'))  108 us
    psum x1, waiting for transfers between devices, shards(): left_panel = lax.psum(dot(buffer, right_basis, ((1,), (0,))), 'col')  102 us
    pallas_call x1, Pallas kernels, chol_inv(): pl.pallas_call(functools.partial(chol_kernel, ridge=ridge), out_shape=jax...  55.3 us
    all_gather x1, waiting for transfers between devices, shards(): gram = lax.all_gather(gram_share, 'col', axis=0, tiled=True)  53 us
    psum x1, waiting for transfers between devices, shards(): cross_panel = lax.psum(partial_cross, ('row', 'rep'))  49.8 us
    dot_general x7, matrix products, dot(): lax.dot_general(left, right, (dims, ((), ())), precision=precision, prefe...  45.3 us
    psum x1, blocking collectives, shards(): lax.psum(jnp.sum(right_panel * right_panel, axis=0, keepdims=True), 'col')  40.3 us
    all_to_all x1, blocking collectives, shards(): lax.all_to_all(slab, 'col', split_axis=1, concat_axis=0, tiled=True)  33.5 us
  transfers between devices with their start and end apart: 5, of which 5 were waited for; matrix products, arithmetic and copies ran while one was open for 3% of the time, Pallas kernels for 10%

profile of v1, /device:TPU:0, one launch (start us, length us, event | category | flops | bytes accessed | tf_op | source)
XLA Modules:
  0.0 527.7 jit_solution(8679010668182062819)
XLA Ops:
  7.2 0.0 copy-start
  7.2 0.0 reduce-scatter.2.cloned.1.call-start
  7.2 2.9 copy.7
  10.2 1.2 copy.6
  11.4 33.5 %all_to_all.19 = f32[64,16,512]{2,0,1:T(8,128)} all-to-all(f32[64,16,512]{2,0,1:T(8,128)S(1)} %copy.6), channel_id=1, replica_groups=mesh['row'=8,'col'=16,'rep'=2] {'col'}, dimensions={1} | all-to-all | bytes 4194304 | tf_op jit(solution)/shard_map/all_to_all | solution.py:107
  44.8 0.0 reduce-scatter.2.cloned.1.call-update
  44.9 0.0 all-reduce.4.cloned.1.call-start
  44.9 14.8 %reduce-scatter.2.cloned.1.call-done = f32[512,512]{1,0:T(8,128)} async-done(((f32[1024,512]{1,0:T(8,128)}), f32[512,512]{1,0:T(8,128)}) %reduce-scatter.2.cloned.1.call-update) | async-done | bytes 1048592 | tf_op jit(solution)/shard_map/reduce_scatter | solution.py:108
  59.7 1.7 add.22
  61.4 0.0 copy-done
  61.5 4.9 fusion.13
  66.3 0.0 all-reduce.4.cloned.1.call-update
  66.4 0.0 all-reduce.6.cloned.1.call-start
  66.4 101.8 %all-reduce.4.cloned.1.call-done = f32[512,1024]{1,0:T(8,128)} async-done(((f32[512,1024]{1,0:T(8,128)}), f32[512,1024]{1,0:T(8,128)}) %all-reduce.4.cloned.1.call-update) | async-done | bytes 2097168 | tf_op jit(solution)/shard_map/psum | solution.py:110
  168.3 3.9 fusion.8
  172.1 0.0 all-reduce.6.cloned.1.call-update
  172.2 0.0 all-gather.2.cloned.1.call-start
  172.2 108.0 %all-reduce.6.cloned.1.call-done = f32[64,1024]{1,0:T(8,128)} async-done(((f32[64,1024]{1,0:T(8,128)}), f32[64,1024]{1,0:T(8,128)}) %all-reduce.6.cloned.1.call-update) | async-done | bytes 262160 | tf_op jit(solution)/shard_map/psum | solution.py:113
  280.2 0.0 all-gather.2.cloned.1.call-update
  280.3 0.0 all-reduce.8.cloned.1.call-start
  280.3 6.4 %fusion.14 = f32[512,1024]{1,0:T(8,128)} fusion(f32[512,512]{1,0:T(8,128)S(1)} %add.22, f32[512,1024]{1,0:T(8,128)} %all-reduce.4.cloned.1.call-done), kind=kOutput, calls=%fused_computation.18 | convolution fusion | flops 3221225472 | bytes 5242880 | tf_op jit(solution)/shard_map/dot_general | solution.py:102
  286.8 53.0 %all-gather.2.cloned.1.call-done.g_ref = f32[1024,1024]{1,0:T(8,128)} async-done(((f32[64,1024]{1,0:T(8,128)}), f32[1024,1024]{1,0:T(8,128)}) %all-gather.2.cloned.1.call-update) | async-done | bytes 4194320 | tf_op jit(solution)/shard_map/all_gather | solution.py:114
  339.8 0.0 all-reduce.8.cloned.1.call-update
  339.8 0.0 copy-start.2
  339.8 2.2 copy-done.2
  342.0 0.0 copy-start.5
  342.0 55.3 %shard_map.58 = f32[1024,1024]{1,0:T(8,128)S(1)} custom-call(f32[1024,1024]{1,0:T(8,128)S(1)} %copy-done.2), custom_call_target="tpu_custom_call" | custom-call | flops 99999997952 | bytes 8388608 | tf_op jit(solution)/shard_map/pallas_call | solution.py:85
  397.4 0.0 copy-start.1
  397.4 1.9 copy-done.1
  399.3 0.0 copy-done.5
  399.3 8.1 %fusion.3 = f32[512,1024]{1,0:T(8,128)} fusion(f32[512,1024]{1,0:T(8,128)S(1)} %copy-done.5, f32[1024,1024]{1,0:T(8,128)S(1)} %shard_map.58), kind=kOutput, calls=%fused_computation.3 | convolution fusion | flops 6444548096 | bytes 8388608 | tf_op jit(solution)/shard_map/dot_general | solution.py:102
  407.4 49.8 %all-reduce.8.cloned.1.call-done = f32[512,1024]{1,0:T(8,128)} async-done(((f32[512,1024]{1,0:T(8,128)}), f32[512,1024]{1,0:T(8,128)}) %all-reduce.8.cloned.1.call-update) | async-done | bytes 2097168 | tf_op jit(solution)/shard_map/psum | solution.py:116
  457.2 10.6 %multiply_reduce_fusion = (f32[1024]{0:T(1024)S(1)}, f32[512,1024]{1,0:T(8,128)}) fusion(f32[512,1024]{1,0:T(8,128)} %all-reduce.8.cloned.1.call-done, f32[1024,1024]{1,0:T(8,128)} %copy-done.1), kind=kOutput, calls=%fused_computation.4 | convolution fusion | flops 6445595648 | bytes 8392704 | tf_op jit(solution)/shard_map/dot_general | solution.py:102
  467.8 40.3 %psum.31 = f32[1,1024]{1,0:T(1,128)S(1)} all-reduce(f32[1,1024]{1,0:T(1,128)S(1)} %bitcast.23), channel_id=1, replica_groups=mesh['row'=8,'col'=16,'rep'=2] {'col'}, use_global_device_ids=true, to_apply=%region_5.6 | all-reduce | flops 1024 | bytes 8192 | tf_op jit(solution)/shard_map/psum | solution.py:120
  508.2 0.0 copy-start.3
  508.2 6.9 %fusion.7 = f32[512,512]{1,0:T(8,128)} fusion(f32[512,512]{1,0:T(8,128)S(1)} %add.22, f32[512,1024]{1,0:T(8,128)} %fusion.3, f32[512,1024]{1,0:T(8,128)} %get-tuple-element.8), kind=kOutput, calls=%fused_computation.9 | convolution fusion | flops 3221749760 | bytes 6291456 | tf_op jit(solution)/shard_map/dot_general | solution.py:102
  515.0 0.0 copy-done.3
  515.0 0.0 copy-start.4
  515.0 0.4 broadcast_divide_fusion
  515.4 1.2 copy-done.4
  516.6 0.0 copy-start.6
  516.6 4.5 convolution_multiply_fusion
  521.1 0.0 copy-done.6
  (1 shorter events, 0.0 us)
Async XLA Ops:
  7.2 54.3 %copy-start = (f32[512,1024]{1,0:T(8,128)S(1)}, f32[512,1024]{1,0:T(8,128)}, u32[]{:S(2)}) copy-start(f32[512,1024]{1,0:T(8,128)} %param.5) | copy-start | bytes 6291460
  7.2 52.5 %reduce-scatter.2.cloned.1.call-start = ((), (), s32[]{:S(2)}) async-start(), calls=%async_computation.2 | async-start | bytes 3145728 | tf_op jit(solution)/shard_map/reduce_scatter | solution.py:108
  44.9 123.4 %all-reduce.4.cloned.1.call-start = ((), (), s32[]{:S(2)}) async-start(), calls=%async_computation.3 | async-start | bytes 4194304 | tf_op jit(solution)/shard_map/psum | solution.py:110
  66.4 213.9 %all-reduce.6.cloned.1.call-start = ((), (), s32[]{:S(2)}) async-start(), calls=%async_computation.4 | async-start | bytes 524288 | tf_op jit(solution)/shard_map/psum | solution.py:113
  172.2 167.6 %all-gather.2.cloned.1.call-start = ((), (), s32[]{:S(2)}) async-start(), calls=%async_computation.5 | async-start | bytes 4456448 | tf_op jit(solution)/shard_map/all_gather | solution.py:114
  280.3 176.9 %all-reduce.8.cloned.1.call-start = ((), (), s32[]{:S(2)}) async-start(), calls=%async_computation.6 | async-start | bytes 4194304 | tf_op jit(solution)/shard_map/psum | solution.py:116
  339.8 2.2 copy-start.2
  342.0 57.3 %copy-start.5 = (f32[512,1024]{1,0:T(8,128)S(1)}, f32[512,1024]{1,0:T(8,128)}, u32[]{:S(2)}) copy-start(f32[512,1024]{1,0:T(8,128)} %all-reduce.4.cloned.1.call-done) | copy-start | bytes 6291460
  397.4 1.9 copy-start.1
  508.2 6.9 %copy-start.3 = (f32[512,1024]{1,0:T(8,128)S(1)}, f32[512,1024]{1,0:T(8,128)}, u32[]{:S(2)}) copy-start(f32[512,1024]{1,0:T(8,128)} %get-tuple-element.8) | copy-start | bytes 6291460
  515.0 1.6 copy-start.4
  516.6 4.5 copy-start.6
Sparse Core Ops, SparseCore 0:
  45.0 14.6 reduce-scatter.1
  66.5 101.7 all-reduce.3
  172.3 107.9 all-reduce.5
  282.8 56.9 all-gather.1
  342.1 115.0 all-reduce.7

commit v2 on v1

--- a/solution.py
+++ b/solution.py
@@ -92,28 +92,340 @@
     )(g)
 
 
+MESH = pl.DeviceIdType.MESH
+
+
+def dot(left, right, dims, precision=HI):
+    return lax.dot_general(left, right, (dims, ((), ())), precision=precision, preferred_element_type=jnp.float32)
+
+
+def remote(src, dst, send, recv, device):
+    return pltpu.make_async_remote_copy(
+        src_ref=src, dst_ref=dst, send_sem=send, recv_sem=recv, device_id=device, device_id_type=MESH
+    )
+
+
+def ring_scatter(piece, half, from_a, from_b, from_left, from_right, pos, left, right, send, recv, started):
+    before, after, across = (pos + 3) % 4, (pos + 1) % 4, (pos + 2) % 4
+    a = remote(half(across, 0), from_a, send.at[0], recv.at[0], left)
+    b = remote(half(across, 1), from_b, send.at[1], recv.at[1], right)
+    a.start()
+    b.start()
+    yield
+    a.wait_recv()
+    half(before, 0)[...] = half(before, 0)[...] + from_a[...]
+    c = remote(piece(before), from_right, send.at[2], recv.at[2], left)
+    c.start()
+    b.wait_recv()
+    half(after, 1)[...] = half(after, 1)[...] + from_b[...]
+    d = remote(piece(after), from_left, send.at[3], recv.at[3], right)
+    d.start()
+    yield
+    c.wait_recv()
+    d.wait_recv()
+    piece(pos)[...] = piece(pos)[...] + (from_left[...] + from_right[...])
+    started += [a, b, c, d]
+
+
+def ring_gather(piece, half, pos, left, right, send, recv, started, done=None):
+    before, after, across = (pos + 3) % 4, (pos + 1) % 4, (pos + 2) % 4
+    a = remote(piece(pos), piece(pos), send.at[0], recv.at[0], left)
+    b = remote(piece(pos), piece(pos), send.at[1], recv.at[1], right)
+    a.start()
+    b.start()
+    if done:
+        done(0, pos)
+    yield
+    a.wait_recv()
+    c = remote(half(after, 0), half(after, 0), send.at[2], recv.at[2], left)
+    c.start()
+    b.wait_recv()
+    d = remote(half(before, 1), half(before, 1), send.at[3], recv.at[3], right)
+    d.start()
+    if done:
+        done(1, after)
+        done(2, before)
+    yield
+    c.wait_recv()
+    d.wait_recv()
+    if done:
+        done(3, across)
+    started += [a, b, c, d]
+
+
+def lockstep(*stages):
+    stages = list(stages)
+    while stages:
+        for stage in list(stages):
+            try:
+                next(stage)
+            except StopIteration:
+                stages.remove(stage)
+
+
+def front_kernel(
+    slab, momentum, basis,
+    gram, buffer, left_panel, cross_half,
+    part, total, landed, panel, from_a, from_b, from_left, from_right, from_a2, from_b2, from_left2, from_right2, full,
+    gram_part, gram_in, gram_slots, gram_sum, gram_all, cross_part, cross_in,
+    part_send, part_recv, land_send, land_recv, ring_send, ring_recv, z_send, z_recv, pair_send, pair_recv,
+):
+    r, c, p = lax.axis_index("row"), lax.axis_index("col"), lax.axis_index("rep")
+    x, y = c // 4, c % 4
+    mate = (r, c, 1 - p)
+    sides = {
+        "x": ((r, ((x + 3) % 4) * 4 + y, p), (r, ((x + 1) % 4) * 4 + y, p)),
+        "y": ((r, x * 4 + (y + 3) % 4, p), (r, x * 4 + (y + 1) % 4, p)),
+    }
+    alone = (c // 8 == p) & (c % 2 == p)
+
+    barrier = pltpu.get_barrier_semaphore()
+    pl.semaphore_signal(barrier, inc=1, device_id=mate, device_id_type=MESH)
+    for axis in ("x", "y"):
+        for side in sides[axis]:
+            pl.semaphore_signal(barrier, inc=1, device_id=side, device_id_type=MESH)
+    for step in range(1, 8):
+        pl.semaphore_signal(barrier, inc=1, device_id=((r + step) % 8, c, p), device_id_type=MESH)
+    for slot in range(8):
+        @pl.when(jnp.logical_not(alone & (8 * p + slot == c)))
+        def _():
+            pl.semaphore_signal(barrier, inc=1, device_id=(r, 8 * p + slot, c % 2), device_id_type=MESH)
+    pl.semaphore_wait(barrier, jnp.where(alone, 19, 20))
+
+    started = []
+
+    first = c // 2
+    copies = []
+    for step in range(8):
+        b = (first + step) % 8
+        cols = pl.ds(pl.multiple_of(512 * (2 * b + 1 - p), 512), 512)
+        copy = remote(slab.at[0, :, cols], part.at[step], part_send.at[step], part_recv.at[step], mate)
+        copy.start()
+        copies.append(copy)
+    started += copies
+    for step in range(8):
+        b = (first + step) % 8
+        d = 2 * b + p
+        copies[step].wait_recv()
+        cols = pl.ds(pl.multiple_of(512 * d, 512), 512)
+        total[step] = part[step] + slab[0, :, cols]
+        own = (d == c) & (c // 8 == p)
+
+        @pl.when(own)
+        def _():
+            landed[c % 8] = total[step]
+
+        @pl.when(jnp.logical_not(own))
+        def _():
+            remote(total.at[step], landed.at[c % 8], land_send.at[step], land_recv.at[c % 8], (r, d, c // 8)).start()
+
+    for slot in range(8):
+        @pl.when(jnp.logical_not(alone & (8 * p + slot == c)))
+        def _():
+            remote(total.at[0], landed.at[slot], land_send.at[0], land_recv.at[slot], (r, 8 * p + slot, c % 2)).wait_recv()
+        buffer[64 * slot : 64 * slot + 64, :] = momentum[64 * slot : 64 * slot + 64, :] + landed[slot]
+
+    across = {"x": (x + 2) % 4, "y": (y + 2) % 4}
+    where = {"x": x, "y": y}
+
+    def product(h):
+        axis = "xy"[h]
+        for t in range(4):
+            if h == 0:
+                rows = buffer[128 * t : 128 * t + 128, :]
+            else:
+                rows = jnp.concatenate([buffer[32 * (4 * u + t) : 32 * (4 * u + t) + 32, :] for u in range(4)], axis=0)
+            got = dot(rows, basis[:, 512 * h : 512 * h + 512], ((1,), (0,)))
+            for u in range(4):
+                panel[h, t, u] = got[32 * u : 32 * u + 32]
+
+    def scatter(h):
+        axis, other = ("x", "y") if h == 0 else ("y", "x")
+        product(h)
+        yield from ring_scatter(
+            lambda i: panel.at[h, i],
+            lambda i, k: panel.at[h, i, pl.ds(2 * k, 2)],
+            from_a.at[h], from_b.at[h], from_left.at[h], from_right.at[h],
+            where[axis], *sides[axis], ring_send.at[h, 0], ring_recv.at[h, 0], started,
+        )
+        yield
+        yield from ring_scatter(
+            lambda i: panel.at[h, where[axis], i],
+            lambda i, k: panel.at[h, where[axis], i, pl.ds(16 * k, 16)],
+            from_a2.at[h], from_b2.at[h], from_left2.at[h], from_right2.at[h],
+            where[other], *sides[other], ring_send.at[h, 1], ring_recv.at[h, 1], started,
+        )
+        full[h, where[axis], where[other]] = panel[h, where[axis], where[other]]
+        yield
+        yield from ring_gather(
+            lambda i: full.at[h, where[axis], i],
+            lambda i, k: full.at[h, where[axis], i, pl.ds(16 * k, 16)],
+            where[other], *sides[other], ring_send.at[h, 2], ring_recv.at[h, 2], started,
+        )
+        yield
+        yield from ring_gather(
+            lambda i: full.at[h, i],
+            lambda i, k: full.at[h, i, pl.ds(2 * k, 2)],
+            where[axis], *sides[axis], ring_send.at[h, 3], ring_recv.at[h, 3], started,
+        )
+
+    lockstep(scatter(0), scatter(1))
+    for u in range(4):
+        for v in range(4):
+            rows = slice(32 * (4 * u + v), 32 * (4 * u + v) + 32)
+            left_panel[rows, 0:512] = full[0, u, v]
+            left_panel[rows, 512:1024] = full[1, v, u]
+
+    rows = pl.ds(pl.multiple_of(128 * (c // 2), 128), 128)
+    mine = left_panel[:, rows]
+    for q in range(2):
+        cols = pl.ds(pl.multiple_of(512 * (c % 2) + 256 * q, 256), 256)
+        gram_part[q] = dot(mine, left_panel[:, cols], ((0,), (0,)))
+    swap = remote(gram_part.at[1 - p], gram_in, pair_send.at[8], pair_recv.at[8], mate)
+    swap.start()
+    started.append(swap)
+
+    for q in range(2):
+        cross_part[q] = dot(buffer[:, 256 * q : 256 * q + 256], left_panel[...], ((0,), (0,)))
+    cross_swap = remote(cross_part.at[1 - p], cross_in, pair_send.at[9], pair_recv.at[9], mate)
+    cross_swap.start()
+    started.append(cross_swap)
+
+    swap.wait_recv()
+    gram_part[p] = gram_part[p] + gram_in[...]
+    moves = []
+    for step in range(1, 8):
+        z = (r + step) % 8
+        piece = gram_part.at[p, pl.ds(pl.multiple_of(16 * z, 16), 16)]
+        move = remote(piece, gram_slots.at[r], z_send.at[0, step], z_recv.at[0, step], (z, c, p))
+        move.start()
+        moves.append(move)
+    gram_slots[r] = gram_part[p, pl.ds(pl.multiple_of(16 * r, 16), 16)]
+    started += moves
+    for move in moves:
+        move.wait_recv()
+    acc = gram_slots[0]
+    for z in range(1, 8):
+        acc = acc + gram_slots[z]
+    h = r // 4
+    f, s = jnp.where(h == 0, x, y), jnp.where(h == 0, y, x)
+    place = gram_all.at[p, h, f, s, pl.ds(pl.multiple_of(16 * (r % 4), 16), 16)]
+    gram_sum[...] = acc
+    place[...] = acc
+    moves = []
+    for step in range(1, 8):
+        move = remote(gram_sum, place, z_send.at[1, step], z_recv.at[1, step], ((r + step) % 8, c, p))
+        move.start()
+        moves.append(move)
+    started += moves
+    for move in moves:
+        move.wait_recv()
+
+    pairs = []
+
+    def gather(h):
+        axis, other = ("x", "y") if h == 0 else ("y", "x")
+        yield from ring_gather(
+            lambda i: gram_all.at[p, h, where[axis], i],
+            lambda i, k: gram_all.at[p, h, where[axis], i, pl.ds(32 * k, 32)],
+            where[other], *sides[other], ring_send.at[h, 4], ring_recv.at[h, 4], started,
+        )
+        yield
+
+        def forward(k, i):
+            view = gram_all.at[p, h, i]
+            copy = remote(view, view, pair_send.at[4 * h + k], pair_recv.at[4 * h + k], mate)
+            copy.start()
+            pairs.append(copy)
+
+        yield from ring_gather(
+            lambda i: gram_all.at[p, h, i],
+            lambda i, k: gram_all.at[p, h, i, pl.ds(2 * k, 2)],
+            where[axis], *sides[axis], ring_send.at[h, 5], ring_recv.at[h, 5], started, forward,
+        )
+
+    lockstep(gather(0), gather(1))
+    for copy in pairs:
+        copy.wait_recv()
+    started += pairs
+    for q in range(2):
+        for u in range(4):
+            for v in range(4):
+                n = 4 * u + v
+                cols = slice(512 * (n % 2) + 256 * q, 512 * (n % 2) + 256 * q + 256)
+                top = 128 * (n // 2)
+                gram[top : top + 64, cols] = gram_all[q, 0, u, v]
+                gram[top + 64 : top + 128, cols] = gram_all[q, 1, v, u]
+
+    cross_swap.wait_recv()
+    cross_half[...] = cross_part[p] + cross_in[...]
+    for copy in started:
+        copy.wait_send()
+    for step in range(8):
+        b = (first + step) % 8
+        d = 2 * b + p
+
+        @pl.when(jnp.logical_not((d == c) & (c // 8 == p)))
+        def _():
+            remote(total.at[step], landed.at[c % 8], land_send.at[step], land_recv.at[c % 8], (r, d, c // 8)).wait_send()
+
+
+def front(gradients, momentum, right_basis):
+    f32 = jnp.float32
+    vmem = pl.BlockSpec(memory_space=pltpu.VMEM)
+    dma = pltpu.SemaphoreType.DMA
+    return pl.pallas_call(
+        front_kernel,
+        out_shape=[
+            jax.ShapeDtypeStruct((N, N), f32),
+            jax.ShapeDtypeStruct((512, 512), f32),
+            jax.ShapeDtypeStruct((512, N), f32),
+            jax.ShapeDtypeStruct((256, N), f32),
+        ],
+        in_specs=[vmem] * 3,
+        out_specs=[vmem] * 4,
+        scratch_shapes=[
+            pltpu.VMEM((8, 64, 512), f32),
+            pltpu.VMEM((8, 64, 512), f32),
+            pltpu.VMEM((8, 64, 512), f32),
+            pltpu.VMEM((2, 4, 4, 32, 512), f32),
+            pltpu.VMEM((2, 2, 32, 512), f32),
+            pltpu.VMEM((2, 2, 32, 512), f32),
+            pltpu.VMEM((2, 4, 32, 512), f32),
+            pltpu.VMEM((2, 4, 32, 512), f32),
+            pltpu.VMEM((2, 16, 512), f32),
+            pltpu.VMEM((2, 16, 512), f32),
+            pltpu.VMEM((2, 32, 512), f32),
+            pltpu.VMEM((2, 32, 512), f32),
+            pltpu.VMEM((2, 4, 4, 32, 512), f32),
+            pltpu.VMEM((2, 128, 256), f32),
+            pltpu.VMEM((128, 256), f32),
+            pltpu.VMEM((8, 16, 256), f32),
+            pltpu.VMEM((16, 256), f32),
+            pltpu.VMEM((2, 2, 4, 4, 64, 256), f32),
+            pltpu.VMEM((2, 256, N), f32),
+            pltpu.VMEM((256, N), f32),
+            dma((8,)), dma((8,)), dma((8,)), dma((8,)),
+            dma((2, 6, 4)), dma((2, 6, 4)),
+            dma((2, 8)), dma((2, 8)),
+            dma((10,)), dma((10,)),
+        ],
+        compiler_params=pltpu.CompilerParams(
+            collective_id=0, has_side_effects=True, vmem_limit_bytes=50 << 20
+        ),
+    )(gradients, momentum, right_basis)
+
+
 EPSILON = 1e-06
 RIDGE = 0.001
 DECAY = 0.95
 D = 8192
 
 
-def dot(left, right, dims, precision=HI):
-    return lax.dot_general(left, right, (dims, ((), ())), precision=precision, preferred_element_type=jnp.float32)
-
-
 def shards(gradients, momentum, right_basis):
-    slab = gradients[0]
-    regrid = lax.all_to_all(slab, "col", split_axis=1, concat_axis=0, tiled=True)
-    summed = lax.psum_scatter(regrid, "rep", scatter_dimension=0, tiled=True)
-    buffer = momentum + summed
-    left_panel = lax.psum(dot(buffer, right_basis, ((1,), (0,))), "col")
-    share = N // lax.axis_size("col")
-    mine = lax.dynamic_slice_in_dim(left_panel, lax.axis_index("col") * share, share, 1)
-    gram_share = lax.psum(dot(mine, left_panel, ((0,), (0,))), ("row", "rep"))
-    gram = lax.all_gather(gram_share, "col", axis=0, tiled=True)
-    partial_cross, gram = lax.optimization_barrier((dot(buffer, left_panel, ((0,), (0,))), gram))
-    cross_panel = lax.psum(partial_cross, ("row", "rep"))
+    gram, buffer, left_panel, cross_half = front(gradients, momentum, right_basis)
+    cross_rows = lax.psum(cross_half, "row")
+    cross_panel = lax.all_gather(cross_rows, "rep", axis=0, tiled=True)
     low = jnp.tril(chol_inv(gram, RIDGE))
     left_unit = dot(left_panel, low, ((1,), (1,)))
     right_panel = dot(cross_panel, low, ((1,), (1,)))

time: 528 us -> 329 us (0.62)
  waiting for transfers between devices: 328 us -> 70.8 us
  Pallas kernels: 55.3 us -> 168 us
  blocking collectives: 73.8 us -> 40 us
  matrix products: 45.3 us -> 27.3 us
    psum x3 -> x1, waiting for transfers between devices: 260 us -> 70.7 us  [shards(): cross_rows = lax.psum(cross_half, 'row')]
    pallas_call x0 -> x1, Pallas kernels: none -> 112 us  [front(): pl.pallas_call(front_kernel, out_shape=[jax.ShapeDtypeStruct((N, N), f32)...]
    all_gather x1, waiting for transfers between devices: 53 us -> 0.01 us  [shards(): cross_panel = lax.all_gather(cross_rows, 'rep', axis=0, tiled=True)]
    all_to_all x1 -> x0, blocking collectives: 33.5 us -> none  [shards(): lax.all_to_all(slab, 'col', split_axis=1, concat_axis=0, tiled=True)]
    dot_general x7 -> x4, matrix products: 45.3 us -> 27.3 us  [dot(): lax.dot_general(left, right, (dims, ((), ())), precision=precision, prefe...]
    reduce_scatter x1 -> x0, waiting for transfers between devices: 14.8 us -> none  [shards(): summed = lax.psum_scatter(regrid, 'rep', scatter_dimension=0, tiled=True)]
  transfers between devices with their start and end apart: 5 -> 2, of which waited for: 5 -> 1; matrix products, arithmetic and copies ran while one was open for 3% -> 2% of each run, Pallas kernels for 10% -> 17%
where the time goes in v2:
time: 329 us; the launch traced here: 328 us
  Pallas kernels  168 us (51%)
  waiting for transfers between devices  70.8 us (22%)
  blocking collectives  40 us (12%)
  matrix products  27.3 us (8%)
  between operations  14.1 us (4%)
  local copies, waits for them, and re-layouts  7.4 us (2%)
    pallas_call x1, Pallas kernels, front(): pl.pallas_call(front_kernel, out_shape=[jax.ShapeDtypeStruct((N, N), f32)...  112 us
    psum x1, waiting for transfers between devices, shards(): cross_rows = lax.psum(cross_half, 'row')  70.7 us
    pallas_call x1, Pallas kernels, chol_inv(): pl.pallas_call(functools.partial(chol_kernel, ridge=ridge), out_shape=jax...  55.2 us
    psum x1, blocking collectives, shards(): lax.psum(jnp.sum(right_panel * right_panel, axis=0, keepdims=True), 'col')  40 us
    dot_general x4, matrix products, dot(): lax.dot_general(left, right, (dims, ((), ())), precision=precision, prefe...  27.3 us
    unnamed x12, local copies, waits for them, and re-layouts  7.4 us
  transfers between devices with their start and end apart: 2, of which 1 were waited for; matrix products, arithmetic and copies ran while one was open for 2% of the time, Pallas kernels for 17%

profile of v2, /device:TPU:0, one launch (start us, length us, event | category | flops | bytes accessed | tf_op | source)
XLA Modules:
  0.0 327.6 jit_solution(18361394722559185873)
XLA Ops:
  7.2 0.0 all-reduce.2.cloned.1.call-start
  7.2 0.0 copy-start.1
  7.2 1.2 copy-done.1
  8.4 112.3 %shard_map.58 = (f32[1024,1024]{1,0:T(8,128)}, f32[512,512]{1,0:T(8,128)S(1)}, f32[512,1024]{1,0:T(8,128)}, f32[256,1024]{1,0:T(8,128)}) custom-call(f32[1,64,8192]{2,1,0:T(8,128)} %slab.1, f32[512,512]{1,0:T(8,128)S(1)} %copy-done.1, f32[512,1024]{1,0:T(8,128)} %basis.1), custom_call_target="tpu_custom_call" | custom-call | tf_op jit(solution)/shard_map/pallas_call | solution.py:377
  120.8 0.0 all-reduce.2.cloned.1.call-update
  120.8 0.2 all-gather.2.cloned.1.call-start
  121.0 70.7 %all-reduce.2.cloned.1.call-done = f32[256,1024]{1,0:T(8,128)} async-done(((f32[256,1024]{1,0:T(8,128)}), f32[256,1024]{1,0:T(8,128)}) %all-reduce.2.cloned.1.call-update) | async-done | bytes 1048592 | tf_op jit(solution)/shard_map/psum | solution.py:427
  191.8 0.0 all-gather.2.cloned.1.call-update
  191.8 0.0 copy-start.2
  191.8 2.2 copy-done.2
  194.0 0.0 copy-start.5
  194.0 55.2 %shard_map.59 = f32[1024,1024]{1,0:T(8,128)S(1)} custom-call(f32[1024,1024]{1,0:T(8,128)S(1)} %copy-done.2), custom_call_target="tpu_custom_call" | custom-call | flops 99999997952 | bytes 8388608 | tf_op jit(solution)/shard_map/pallas_call | solution.py:85
  249.2 0.0 copy-start
  249.2 1.9 copy-done
  251.1 0.0 copy-done.5
  251.1 8.1 %fusion.3 = f32[512,1024]{1,0:T(8,128)} fusion(f32[512,1024]{1,0:T(8,128)S(1)} %copy-done.5, f32[1024,1024]{1,0:T(8,128)S(1)} %shard_map.59), kind=kOutput, calls=%fused_computation.3 | convolution fusion | flops 6444548096 | bytes 8388608 | tf_op jit(solution)/shard_map/dot_general | solution.py:99
  259.2 0.0 all-gather.2.cloned.1.call-done
  259.2 10.1 %multiply_reduce_fusion = (f32[1024]{0:T(1024)S(1)}, f32[512,1024]{1,0:T(8,128)S(1)}) fusion(f32[512,1024]{1,0:T(8,128)} %all-gather.2.cloned.1.call-done, f32[1024,1024]{1,0:T(8,128)} %copy-done), kind=kOutput, calls=%fused_computation.4 | convolution fusion | flops 6445595648 | bytes 8392704 | tf_op jit(solution)/shard_map/dot_general | solution.py:99
  269.3 40.0 %psum.15 = f32[1,1024]{1,0:T(1,128)S(1)} all-reduce(f32[1,1024]{1,0:T(1,128)S(1)} %bitcast.8), channel_id=1, replica_groups=mesh['row'=8,'col'=16,'rep'=2] {'col'}, use_global_device_ids=true, to_apply=%region_2.3 | all-reduce | flops 1024 | bytes 8192 | tf_op jit(solution)/shard_map/psum | solution.py:432
  309.3 0.0 copy-start.3
  309.4 0.3 broadcast_divide_fusion
  309.6 0.0 copy-start.4
  309.6 2.1 copy-done.3
  311.7 4.5 %fusion.7 = f32[512,512]{1,0:T(8,128)} fusion(f32[512,512]{1,0:T(8,128)S(1)} %get-tuple-element.7, f32[512,1024]{1,0:T(8,128)S(1)} %copy-done.3, f32[512,1024]{1,0:T(8,128)S(1)} %get-tuple-element.12), kind=kOutput, calls=%fused_computation.9 | convolution fusion | flops 3221749760 | bytes 6291456 | tf_op jit(solution)/shard_map/dot_general | solution.py:99
  316.2 0.0 copy-done.4
  316.2 4.5 %convolution_multiply_fusion = f32[512,512]{1,0:T(8,128)} fusion(f32[512,1024]{1,0:T(8,128)S(1)} %copy-done.3, f32[512,1024]{1,0:T(8,128)S(1)} %broadcast_divide_fusion), kind=kOutput, calls=%fused_computation.7 | convolution fusion | flops 3221487616 | bytes 5242880 | tf_op jit(solution)/shard_map/dot_general | solution.py:99
  (1 shorter events, 0.0 us)
Async XLA Ops:
  7.2 184.6 %all-reduce.2.cloned.1.call-start = ((), (), s32[]{:S(2)}) async-start(), calls=%async_computation | async-start | bytes 2097152 | tf_op jit(solution)/shard_map/psum | solution.py:427
  7.2 1.2 copy-start.1
  120.8 138.4 %all-gather.2.cloned.1.call-start = ((), (), s32[]{:S(2)}) async-start(), calls=%async_computation.1 | async-start | bytes 3145728 | tf_op jit(solution)/shard_map/all_gather | solution.py:428
  191.8 2.2 copy-start.2
  194.0 57.1 %copy-start.5 = (f32[512,1024]{1,0:T(8,128)S(1)}, f32[512,1024]{1,0:T(8,128)}, u32[]{:S(2)}) copy-start(f32[512,1024]{1,0:T(8,128)} %get-tuple-element.8) | copy-start | bytes 6291460
  249.2 1.9 copy-start
  309.3 2.3 copy-start.3
  309.6 6.6 %copy-start.4 = (f32[512,1024]{1,0:T(8,128)}, f32[512,1024]{1,0:T(8,128)S(1)}, u32[]{:S(2)}) copy-start(f32[512,1024]{1,0:T(8,128)S(1)} %broadcast_divide_fusion) | copy-start | bytes 6291460
Sparse Core Ops, SparseCore 0:
  120.9 70.8 all-reduce.1
  193.6 14.1 all-gather.1

commit v3 on v2

--- a/solution.py
+++ b/solution.py
@@ -1,7 +1,8 @@
 import functools
 import math
 
-import jax, jax.numpy as jnp
+import jax
+import jax.numpy as jnp
 from jax import lax
 from jax.experimental import pallas as pl
 from jax.experimental.pallas import tpu as pltpu
@@ -10,99 +11,213 @@
 N = 1024
 NB = 128
 HI = lax.Precision.HIGHEST
-
-
-def factor_block(rows):
-    nr = len(rows)
-    rows = list(rows)
-    lane = lax.broadcasted_iota(jnp.int32, (8, NB), 1)
-    sub = lax.broadcasted_iota(jnp.int32, (8, NB), 0)
-
-    def lanes(v, j):
-        return jnp.broadcast_to(v[:, j : j + 1], (8, NB))
-
-    def subs(v, k):
-        return jnp.broadcast_to(v[k : k + 1, :], (8, NB))
-
-    for J in range(nr):
-        blk = (lane >= 8 * J) & (lane < 8 * J + 8)
-        V = rows[J]
-        C = [lanes(V, 8 * J + k) for k in range(8)]
-        D = {i: [lanes(rows[i], 8 * J + k) for k in range(8)] for i in range(J + 1, nr)}
-        V = jnp.where(blk, jnp.where(lane - 8 * J == sub, 1.0, 0.0), V)
-        for i in range(J + 1, nr):
-            rows[i] = jnp.where(blk, 0.0, rows[i])
-        for k in range(8):
-            s = lax.rsqrt(subs(C[k], k))
-            vk = subs(V, k) * s
-            f = jnp.where(sub > k, C[k] * s, 0.0)
-            V = jnp.where(sub == k, vk, V - f * vk)
-            ck = {}
-            for q in range(k + 1, 8):
-                ck[q] = subs(C[q], k) * s
-                C[q] = C[q] - f * ck[q]
-            for i in range(J + 1, nr):
-                fi = D[i][k] * s
-                rows[i] = rows[i] - fi * vk
-                for q in range(k + 1, 8):
-                    D[i][q] = D[i][q] - fi * ck[q]
-        rows[J] = V
-    return rows
-
-
-def chol_kernel(g_ref, x_ref, ridge, prec=HI):
-    nb = N // NB
-    r = lax.broadcasted_iota(jnp.int32, (NB, NB), 0)
-    c = lax.broadcasted_iota(jnp.int32, (NB, NB), 1)
-    x_ref[...] = g_ref[...]
-
-    def step(k, _):
-        kr = pl.ds(pl.multiple_of(k * NB, NB), NB)
-        rows = [x_ref[pl.ds(pl.multiple_of(k * NB + 8 * i, 8), 8), kr] for i in range(NB // 8)]
-        eye8 = [jnp.where(lax.broadcasted_iota(jnp.int32, (8, NB), 0) + 8 * i == lax.broadcasted_iota(jnp.int32, (8, NB), 1), ridge, 0.0) for i in range(NB // 8)]
-        rows = [a + b for a, b in zip(rows, eye8)]
-        rows = factor_block(rows)
-        res = jnp.concatenate(rows, axis=0)
-        dinv = jnp.where(r >= c, res, 0.0)
-        x_ref[kr, kr] = jnp.where(r == c, 1.0, 0.0)
-        rs = lax.dot_general(dinv, x_ref[kr, :], (((1,), (0,)), ((), ())), precision=prec, preferred_element_type=jnp.float32)
-        x_ref[kr, :] = rs
-
-        def trail(i, _):
-            ir = pl.ds(pl.multiple_of(i * NB, NB), NB)
-            f = x_ref[kr, ir]
-            x_ref[ir, kr] = jnp.zeros((NB, NB), jnp.float32)
-            x_ref[ir, :] = x_ref[ir, :] - lax.dot_general(f, x_ref[kr, :], (((0,), (0,)), ((), ())), precision=prec, preferred_element_type=jnp.float32)
-            return 0
-
-        lax.fori_loop(k + 1, nb, trail, 0)
-        return 0
-
-    lax.fori_loop(0, nb, step, 0)
-
-
-def chol_inv(g, ridge):
-    return pl.pallas_call(
-        functools.partial(chol_kernel, ridge=ridge),
-        out_shape=jax.ShapeDtypeStruct((N, N), jnp.float32),
-        in_specs=[pl.BlockSpec(memory_space=pltpu.VMEM)],
-        out_specs=pl.BlockSpec(memory_space=pltpu.VMEM),
-        cost_estimate=pl.CostEstimate(flops=100_000_000_000, bytes_accessed=8 << 20, transcendentals=0),
-        compiler_params=pltpu.CompilerParams(vmem_limit_bytes=40 << 20),
-    )(g)
-
-
+EPSILON = 1e-06
+RIDGE = 0.001
+DECAY = 0.95
+D = 8192
 MESH = pl.DeviceIdType.MESH
 
 
 def dot(left, right, dims, precision=HI):
     return lax.dot_general(left, right, (dims, ((), ())), precision=precision, preferred_element_type=jnp.float32)
+
+
+def split(a):
+    high = a.astype(jnp.bfloat16)
+    return high, (a - high.astype(jnp.float32)).astype(jnp.bfloat16)
+
+
+def dot3(left, right, dims):
+    def one(a, b):
+        return lax.dot_general(a, b, (dims, ((), ())), preferred_element_type=jnp.float32)
+
+    return one(left[0], right[0]) + (one(left[0], right[1]) + one(left[1], right[0]))
 
 
 def remote(src, dst, send, recv, device):
     return pltpu.make_async_remote_copy(
         src_ref=src, dst_ref=dst, send_sem=send, recv_sem=recv, device_id=device, device_id_type=MESH
     )
+
+
+def factor_block(rest):
+    lane = lax.broadcasted_iota(jnp.int32, (8, NB), 1)
+    sub = lax.broadcasted_iota(jnp.int32, (8, NB), 0)
+    done = []
+    for base in range(0, NB, 8):
+        top, rest = rest[:8], rest[8:]
+        n = rest.shape[0]
+        inside = (lane >= base) & (lane < base + 8)
+        pivots = [jnp.broadcast_to(top[:, base + k : base + k + 1], (8, NB)) for k in range(8)]
+        top = jnp.where(inside, jnp.where(lane - base == sub, 1.0, 0.0), top)
+        if n:
+            below = [jnp.broadcast_to(rest[:, base + k : base + k + 1], (n, NB)) for k in range(8)]
+            wide = lax.broadcasted_iota(jnp.int32, (n, NB), 1)
+            rest = jnp.where((wide >= base) & (wide < base + 8), 0.0, rest)
+        for k in range(8):
+            scale = lax.rsqrt(pivots[k][k : k + 1, :])
+            row = top[k : k + 1, :] * scale
+            factor = jnp.where(sub > k, pivots[k] * scale, 0.0)
+            top = jnp.where(sub == k, row, top - factor * row)
+            cross = {}
+            for q in range(k + 1, 8):
+                cross[q] = pivots[q][k : k + 1, :] * scale
+                pivots[q] = pivots[q] - factor * cross[q]
+            if n:
+                lower = below[k] * scale
+                rest = rest - lower * row
+                for q in range(k + 1, 8):
+                    below[q] = below[q] - lower * cross[q]
+        done.append(top)
+    return jnp.concatenate(done, axis=0)
+
+
+def chol_steps(x, begin, end):
+    r = lax.broadcasted_iota(jnp.int32, (NB, NB), 0)
+    c = lax.broadcasted_iota(jnp.int32, (NB, NB), 1)
+
+    def step(k, _):
+        own = pl.ds(pl.multiple_of(k * NB, NB), NB)
+        block = factor_block(x[own, own] + jnp.where(r == c, RIDGE, 0.0))
+        x[own, own] = jnp.where(r == c, 1.0, 0.0)
+        x[own, :] = dot(jnp.where(r >= c, block, 0.0), x[own, :], ((1,), (0,)))
+
+        def trail(i, _):
+            rows = pl.ds(pl.multiple_of(i * NB, NB), NB)
+            factor = x[own, rows]
+            x[rows, own] = jnp.zeros((NB, NB), jnp.float32)
+            x[rows, :] = x[rows, :] - dot(factor, x[own, :], ((0,), (0,)))
+            return 0
+
+        lax.fori_loop(k + 1, N // NB, trail, 0)
+        return 0
+
+    lax.fori_loop(begin, end, step, 0)
+
+
+def middle_kernel(
+    gram, cross_half, left_panel,
+    left_unit, right_panel, squares,
+    x, slots, total, half_all, mate_half, own_squares, square_slots,
+    z_send, z_recv, pair_send, pair_recv, col_send, col_recv,
+):
+    r, c, p = lax.axis_index("row"), lax.axis_index("col"), lax.axis_index("rep")
+    mate = (r, c, 1 - p)
+    barrier = pltpu.get_barrier_semaphore()
+    pl.semaphore_signal(barrier, inc=1, device_id=mate, device_id_type=MESH)
+    for step in range(1, 8):
+        pl.semaphore_signal(barrier, inc=1, device_id=((r + step) % 8, c, p), device_id_type=MESH)
+    for step in range(1, 16):
+        pl.semaphore_signal(barrier, inc=1, device_id=(r, (c + step) % 16, p), device_id_type=MESH)
+    pl.semaphore_wait(barrier, 23)
+
+    started = []
+    moves = []
+    for step in range(1, 8):
+        z = (r + step) % 8
+        piece = cross_half.at[pl.ds(pl.multiple_of(32 * z, 32), 32)]
+        move = remote(piece, slots.at[r], z_send.at[0, step], z_recv.at[0, step], (z, c, p))
+        move.start()
+        moves.append(move)
+    slots[r] = cross_half[pl.ds(pl.multiple_of(32 * r, 32), 32), :]
+    started += moves
+
+    x[...] = gram[...]
+    chol_steps(x, 0, 4)
+
+    for move in moves:
+        move.wait_recv()
+    acc = slots[0]
+    for z in range(1, 8):
+        acc = acc + slots[z]
+    total[...] = acc
+    place = half_all.at[pl.ds(pl.multiple_of(32 * r, 32), 32)]
+    place[...] = acc
+    moves = []
+    for step in range(1, 8):
+        move = remote(total, place, z_send.at[1, step], z_recv.at[1, step], ((r + step) % 8, c, p))
+        move.start()
+        moves.append(move)
+    started += moves
+
+    chol_steps(x, 4, 7)
+
+    for move in moves:
+        move.wait_recv()
+    swap = remote(half_all, mate_half, pair_send, pair_recv, mate)
+    swap.start()
+    started.append(swap)
+
+    chol_steps(x, 7, 8)
+
+    rows = lax.broadcasted_iota(jnp.int32, (256, 256), 0)
+    cols = lax.broadcasted_iota(jnp.int32, (256, 256), 1)
+    low = []
+    for j in range(4):
+        band = x[256 * j : 256 * j + 256, : 256 * j + 256]
+        corner = jnp.where(rows >= cols, band[:, 256 * j :], 0.0)
+        low.append(split(jnp.concatenate([band[:, : 256 * j], corner], axis=1) if j else corner))
+
+    def solve(panel, out, at):
+        high, rest = split(panel)
+        for j in range(4):
+            n = 256 * j + 256
+            out[at, 256 * j : n] = dot3((high[:, :n], rest[:, :n]), low[j], ((1,), (1,)))
+
+    swap.wait_recv()
+    for q in range(2):
+        @pl.when(p == q)
+        def _():
+            solve(half_all[...], right_panel, slice(256 * q, 256 * q + 256))
+            solve(mate_half[...], right_panel, slice(256 - 256 * q, 512 - 256 * q))
+    v = right_panel[...]
+    sums = jnp.sum(v * v, axis=0, keepdims=True)
+    for k in range(8):
+        own_squares[k : k + 1, :] = sums[:, 128 * k : 128 * k + 128]
+    square_slots[c] = own_squares[...]
+    moves = []
+    for step in range(1, 16):
+        move = remote(own_squares, square_slots.at[c], col_send.at[step], col_recv.at[step], (r, (c + step) % 16, p))
+        move.start()
+        moves.append(move)
+    started += moves
+    solve(left_panel[...], left_unit, slice(0, 512))
+    for move in moves:
+        move.wait_recv()
+    acc = square_slots[0]
+    for i in range(1, 16):
+        acc = acc + square_slots[i]
+    for k in range(8):
+        squares[:, 128 * k : 128 * k + 128] = acc[k : k + 1, :]
+    for move in started:
+        move.wait_send()
+
+
+def middle(gram, cross_half, left_panel):
+    f32 = jnp.float32
+    vmem = pl.BlockSpec(memory_space=pltpu.VMEM)
+    dma = pltpu.SemaphoreType.DMA
+    return pl.pallas_call(
+        middle_kernel,
+        out_shape=[
+            jax.ShapeDtypeStruct((512, N), f32),
+            jax.ShapeDtypeStruct((512, N), f32),
+            jax.ShapeDtypeStruct((1, N), f32),
+        ],
+        in_specs=[vmem] * 3,
+        out_specs=[vmem] * 3,
+        scratch_shapes=[
+            pltpu.VMEM((N, N), f32),
+            pltpu.VMEM((8, 32, N), f32),
+            pltpu.VMEM((32, N), f32),
+            pltpu.VMEM((256, N), f32),
+            pltpu.VMEM((256, N), f32),
+            pltpu.VMEM((8, 128), f32),
+            pltpu.VMEM((16, 8, 128), f32),
+            dma((2, 8)), dma((2, 8)), dma, dma, dma((16,)), dma((16,)),
+        ],
+        compiler_params=pltpu.CompilerParams(collective_id=1, has_side_effects=True, vmem_limit_bytes=50 << 20),
+    )(gram, cross_half, left_panel)
 
 
 def ring_scatter(piece, half, from_a, from_b, from_left, from_right, pos, left, right, send, recv, started):
@@ -416,23 +531,13 @@
     )(gradients, momentum, right_basis)
 
 
-EPSILON = 1e-06
-RIDGE = 0.001
-DECAY = 0.95
-D = 8192
-
-
 def shards(gradients, momentum, right_basis):
     gram, buffer, left_panel, cross_half = front(gradients, momentum, right_basis)
-    cross_rows = lax.psum(cross_half, "row")
-    cross_panel = lax.all_gather(cross_rows, "rep", axis=0, tiled=True)
-    low = jnp.tril(chol_inv(gram, RIDGE))
-    left_unit = dot(left_panel, low, ((1,), (1,)))
-    right_panel = dot(cross_panel, low, ((1,), (1,)))
-    squares = lax.psum(jnp.sum(right_panel * right_panel, axis=0, keepdims=True), "col")
+    left_unit, right_panel, squares = middle(gram, cross_half, left_panel)
     new_basis = right_panel / jnp.sqrt(squares + EPSILON)
-    new_momentum = buffer - (1.0 - DECAY) * dot(left_unit, right_panel, ((1,), (1,)))
-    update = (D / math.sqrt(N)) * dot(left_unit, new_basis, ((1,), (1,)))
+    fine = lax.Precision.HIGH
+    new_momentum = buffer - (1.0 - DECAY) * dot(left_unit, right_panel, ((1,), (1,)), fine)
+    update = (D / math.sqrt(N)) * dot(left_unit, new_basis, ((1,), (1,)), fine)
     return (new_momentum, new_basis, update)
 
 

time: 329 us -> 204 us (0.62)
  waiting for transfers between devices: 70.8 us -> 0 us
  blocking collectives: 40 us -> 0 us
  Pallas kernels: 168 us -> 192 us
  matrix products: 27.3 us -> 7.46 us
  between operations: 14.1 us -> 0.69 us
  local copies, waits for them, and re-layouts: 7.4 us -> 1.23 us
    psum x1 -> x0, waiting for transfers between devices: 70.7 us -> none  [shards(): cross_rows = lax.psum(cross_half, 'row')]
    psum x1 -> x0, blocking collectives: 40 us -> none  [shards(): lax.psum(jnp.sum(right_panel * right_panel, axis=0, keepdims=True), 'col')]
    pallas_call x1, Pallas kernels: 55.2 us -> 79.6 us  [middle(): pl.pallas_call(middle_kernel, out_shape=[jax.ShapeDtypeStruct((512, N), f...]
    dot_general x4 -> x2, matrix products: 27.3 us -> 7.46 us  [dot(): lax.dot_general(left, right, (dims, ((), ())), precision=precision, prefe...]
    unnamed x12 -> x6, local copies, waits for them, and re-layouts: 7.4 us -> 1.23 us
  transfers between devices with their start and end apart: 2 -> 0, of which waited for: 1 -> 0; matrix products, arithmetic and copies ran while one was open for 2% -> 0% of each run, Pallas kernels for 17% -> 0%
where the time goes in v3:
time: 204 us; the launch traced here: 202 us
  Pallas kernels  192 us (94%)
  matrix products  7.46 us (4%)
    pallas_call x1, Pallas kernels, front(): pl.pallas_call(front_kernel, out_shape=[jax.ShapeDtypeStruct((N, N), f32)...  112 us
    pallas_call x1, Pallas kernels, middle(): pl.pallas_call(middle_kernel, out_shape=[jax.ShapeDtypeStruct((512, N), f...  79.6 us
    dot_general x2, matrix products, dot(): lax.dot_general(left, right, (dims, ((), ())), precision=precision, prefe...  7.46 us

profile of v3, /device:TPU:0, one launch (start us, length us, event | category | flops | bytes accessed | tf_op | source)
XLA Modules:
  0.0 201.6 jit_solution(12319700383311104712)
XLA Ops:
  0.6 0.0 copy-start
  0.6 1.2 copy-done
  1.9 112.2 %shard_map.58 = (f32[1024,1024]{1,0:T(8,128)}, f32[512,512]{1,0:T(8,128)S(1)}, f32[512,1024]{1,0:T(8,128)}, f32[256,1024]{1,0:T(8,128)S(1)}) custom-call(f32[1,64,8192]{2,1,0:T(8,128)} %slab.1, f32[512,512]{1,0:T(8,128)S(1)} %copy-done, f32[512,1024]{1,0:T(8,128)} %basis.1), custom_call_target="tpu_custom_call" | custom-call | tf_op jit(solution)/shard_map/pallas_call | solution.py:492
  114.1 79.6 %shard_map.59 = (f32[512,1024]{1,0:T(8,128)S(1)}, f32[512,1024]{1,0:T(8,128)}, f32[1,1024]{1,0:T(1,128)S(1)}) custom-call(f32[1024,1024]{1,0:T(8,128)} %get-tuple-element.11.gram, f32[256,1024]{1,0:T(8,128)S(1)} %get-tuple-element.12.cross_half, f32[512,1024]{1,0:T(8,128)} %get-tuple-element.13.left_panel), custom_call_target="tpu_custom_call" | custom-call | tf_op jit(solution)/shard_map/pallas_call | solution.py:200
  193.7 0.0 copy-start.1
  193.8 4.6 %fusion = f32[512,512]{1,0:T(8,128)} fusion(f32[512,512]{1,0:T(8,128)S(1)} %get-tuple-element.10, f32[512,1024]{1,0:T(8,128)S(1)} %get-tuple-element.14, f32[512,1024]{1,0:T(8,128)} %get-tuple-element.15), kind=kOutput, calls=%fused_computation.2 | convolution fusion | flops 1611137024 | bytes 6291456 | tf_op jit(solution)/shard_map/dot_general | solution.py:22
  198.3 0.0 copy-done.1
  198.3 0.4 broadcast_divide_fusion
  198.7 0.0 copy-start.2
  198.7 2.9 %convolution_multiply_fusion = f32[512,512]{1,0:T(8,128)} fusion(f32[512,1024]{1,0:T(8,128)S(1)} %get-tuple-element.14, f32[512,1024]{1,0:T(8,128)S(1)} %broadcast_divide_fusion), kind=kOutput, calls=%fused_computation | convolution fusion | flops 1610874880 | bytes 5242880 | tf_op jit(solution)/shard_map/dot_general | solution.py:22
  201.6 0.0 copy-done.2
  (1 shorter events, 0.0 us)
Async XLA Ops:
  0.6 1.2 copy-start
  193.7 4.6 %copy-start.1 = (f32[512,1024]{1,0:T(8,128)S(1)}, f32[512,1024]{1,0:T(8,128)}, u32[]{:S(2)}) copy-start(f32[512,1024]{1,0:T(8,128)} %get-tuple-element.15) | copy-start | bytes 6291460
  198.7 2.9 %copy-start.2 = (f32[512,1024]{1,0:T(8,128)}, f32[512,1024]{1,0:T(8,128)S(1)}, u32[]{:S(2)}) copy-start(f32[512,1024]{1,0:T(8,128)S(1)} %broadcast_divide_fusion) | copy-start | bytes 6291460
